TPU v7x, 512 devices: a whole 4x4x16 slice. The times are simulated.
512 devices in a mesh: dp: 8 (over z_lo), pipe: 4 (over x), seq: 16 (over z_hi, y, core).
Axes of the slice: x: 4, y: 4, z: 16 (z_hi: 2, z_lo: 8; z = z_hi * 8 + z_lo), core: 2. Of those that a mesh axis runs over, the one named last changes fastest.
Arguments:
- queries: bfloat16 [4, 8, 2048, 2048], P('pipe', 'dp', 'seq'), may hold values from -6 to 6
- keys: bfloat16 [4, 8, 2048, 512], P('pipe', 'dp', 'seq'), may hold values from -6 to 6
- values: bfloat16 [4, 8, 2048, 512], P('pipe', 'dp', 'seq'), may hold values from -6 to 6
- grad_next: bfloat16 [4, 8, 2048, 2048], P('pipe', 'dp', 'seq'), may hold values from -6 to 6
- normed: bfloat16 [4, 8, 2048, 4096], P('pipe', 'dp', 'seq'), may hold values from -6 to 6
- value_weight: bfloat16 [4, 4096, 512], P('pipe', 'seq'), may hold values from -0.09375 to 0.09375
Outputs:
- grad_queries: bfloat16 [4, 8, 2048, 2048], P('pipe', 'dp', 'seq')
- grad_keys: bfloat16 [4, 8, 2048, 512], P('pipe', 'dp', 'seq')
- grad_normed: bfloat16 [4, 8, 2048, 4096], P('pipe', 'dp', 'seq')
- grad_value_weight: float32 [4, 4096, 512], P('pipe', 'seq')
All inputs are finite; a program needn't handle non-finite values.
Results may differ from a plain program's by a relative error of at most 0.019.
Values may be sent and summed in bfloat16 or wider, within the bound.
A program may use at most 64 MiB of HBM per device.

v0:
```python
import jax
import jax.numpy as jnp
from jax import lax
from jax.sharding import PartitionSpec as P

HEAD = 128
HQ = 16
masked_value = -1e30


def passed_along(block, axis, distance):
    devices = range(lax.axis_size(axis))
    route = [((i - distance) % len(devices), i) for i in devices]
    return lax.ppermute(block, axis, route)


def attend(query_head, key_head, value_head, upstream_head):
    length = query_head.shape[0]
    block_rows = min(512, length)
    factor = HEAD ** (-0.5)
    query_parts = []
    grad_key = jnp.zeros((length, HEAD), jnp.float32)
    grad_value = jnp.zeros((length, HEAD), jnp.float32)
    for block_index in range(length // block_rows):
        first_row = block_index * block_rows
        finish = first_row + block_rows
        query_block = query_head[first_row:finish]
        upstream_block = upstream_head[first_row:finish]
        key_prefix = key_head[:finish]
        value_prefix = value_head[:finish]
        row_pos = first_row + jnp.arange(block_rows, dtype=jnp.int32)[:, None]
        col_pos = jnp.arange(finish, dtype=jnp.int32)[None, :]
        scores = jnp.where(
            col_pos <= row_pos,
            lax.dot_general(
                query_block,
                key_prefix,
                (((1,), (1,)), ((), ())),
                preferred_element_type=jnp.float32,
            )
            * factor,
            masked_value,
        )
        row_top = jnp.max(scores, axis=1, keepdims=True)
        row_total = jnp.sum(jnp.exp(scores - row_top), axis=1, keepdims=True)
        probs_half = (jnp.exp(scores - row_top) / row_total).astype(jnp.bfloat16)
        attn_out = jnp.dot(probs_half, value_prefix, preferred_element_type=jnp.float32)
        row_delta = jnp.sum(upstream_block.astype(jnp.float32) * attn_out, axis=1, keepdims=True)
        grad_probs = lax.dot_general(
            upstream_block,
            value_prefix,
            (((1,), (1,)), ((), ())),
            preferred_element_type=jnp.float32,
        )
        grad_scores = (jnp.exp(scores - row_top) / row_total * (grad_probs - row_delta)).astype(
            jnp.bfloat16
        )
        query_parts.append(
            jnp.dot(grad_scores, key_prefix, preferred_element_type=jnp.float32) * factor
        )
        key_part = (
            lax.dot_general(
                grad_scores,
                query_block,
                (((0,), (0,)), ((), ())),
                preferred_element_type=jnp.float32,
            )
            * factor
        )
        value_part = lax.dot_general(
            probs_half, upstream_block, (((0,), (0,)), ((), ())), preferred_element_type=jnp.float32
        )
        grad_key = grad_key.at[:finish].add(key_part)
        grad_value = grad_value.at[:finish].add(value_part)
    return (jnp.concatenate(query_parts, axis=0), grad_key, grad_value)


def local(queries, keys, values, grad_next, normed, value_weight):
    query_rows = queries[0, 0]
    key_rows = keys[0, 0]
    value_rows = values[0, 0]
    normed_rows = normed[0, 0]
    value_proj = value_weight[0]
    upstream = passed_along(grad_next[0, 0], "pipe", -1)
    tokens = query_rows.shape[0]
    kv_heads = key_rows.shape[1] // HEAD
    repeats = HQ // kv_heads

    def widen(source):
        spread = jnp.broadcast_to(
            source.reshape(tokens, kv_heads, 1, HEAD), (tokens, kv_heads, repeats, HEAD)
        )
        return spread.reshape(tokens, kv_heads * repeats * HEAD)

    query_cols, key_cols, value_cols, upstream_cols = (
        lax.all_to_all(query_rows, "seq", split_axis=1, concat_axis=0, tiled=True),
        lax.all_to_all(widen(key_rows), "seq", split_axis=1, concat_axis=0, tiled=True),
        lax.all_to_all(widen(value_rows), "seq", split_axis=1, concat_axis=0, tiled=True),
        lax.all_to_all(upstream, "seq", split_axis=1, concat_axis=0, tiled=True),
    )
    head_grads = [attend(query_cols, key_cols, value_cols, upstream_cols)]
    query_terms = jnp.concatenate([entry[0] for entry in head_grads], axis=1).astype(jnp.bfloat16)
    key_terms = jnp.concatenate([entry[1] for entry in head_grads], axis=1).astype(jnp.bfloat16)
    value_terms = jnp.concatenate([entry[2] for entry in head_grads], axis=1).astype(jnp.bfloat16)
    back_query, back_key, back_value = (
        lax.all_to_all(query_terms, "seq", split_axis=0, concat_axis=1, tiled=True),
        lax.all_to_all(key_terms, "seq", split_axis=0, concat_axis=1, tiled=True),
        lax.all_to_all(value_terms, "seq", split_axis=0, concat_axis=1, tiled=True),
    )

    def grouped(head_terms):
        summed = head_terms.astype(jnp.float32).reshape(tokens, kv_heads, repeats, HEAD).sum(axis=2)
        return summed.reshape(tokens, kv_heads * HEAD).astype(jnp.bfloat16)

    key_grad_rows = grouped(back_key)
    value_grad_rows = grouped(back_value)
    normed_cols = lax.all_to_all(normed_rows, "seq", split_axis=1, concat_axis=0, tiled=True)
    all_value_grads = lax.all_gather(value_grad_rows, "seq", axis=0, tiled=True)
    weight_term = lax.dot_general(
        normed_cols, all_value_grads, (((0,), (0,)), ((), ())), preferred_element_type=jnp.float32
    )
    weight_grad = lax.psum(weight_term.astype(jnp.bfloat16), "dp").astype(jnp.float32)
    full_rows = lax.dot_general(
        value_grad_rows,
        lax.all_gather(value_proj, "seq", axis=0, tiled=True),
        (((1,), (1,)), ((), ())),
        preferred_element_type=jnp.float32,
    )
    input_grad = full_rows.astype(jnp.bfloat16)
    return (
        back_query[None, None],
        key_grad_rows[None, None],
        input_grad[None, None],
        weight_grad[None],
    )


def solution(mesh):
    placed = (
        P("pipe", "dp", "seq", None),
        P("pipe", "dp", "seq", None),
        P("pipe", "dp", "seq", None),
        P("pipe", "dp", "seq", None),
        P("pipe", "dp", "seq", None),
        P("pipe", "seq", None),
    )
    return jax.shard_map(
        local,
        mesh=mesh,
        in_specs=placed,
        out_specs=(
            P("pipe", "dp", "seq", None),
            P("pipe", "dp", "seq", None),
            P("pipe", "dp", "seq", None),
            P("pipe", "seq", None),
        ),
        check_vma=False,
    )
```

profile of v0, /device:TPU:2, one launch (start us, length us, event | category | flops | bytes accessed | tf_op | source)
XLA Modules:
  0.0 549.3 jit_solution(11475916848880484211)
XLA Ops:
  7.2 1.0 broadcast_in_dim.33
  9.1 17.8 %all-to-all-start.1 = ((bf16[128,16,128]{2,0,1:T(8,128)(2,1)}), bf16[128,16,128]{2,0,1:T(8,128)(2,1)S(1)}, u32[]{:S(2)}, u32[]{:S(2)}) async-start(bf16[128,16,128]{2,0,1:T(8,128)(2,1)} %bitcast.3), calls=%async_computation.1 | async-start | bytes 1048576 | tf_op jit(solution)/shard_map/all_to_all | solution.py:97
  27.0 1.0 copy.50
  28.0 19.1 %all-to-all-done.1 = bf16[128,16,128]{2,0,1:T(8,128)(2,1)S(1)} async-done(((bf16[128,16,128]{2,0,1:T(8,128)(2,1)}), bf16[128,16,128]{2,0,1:T(8,128)(2,1)S(1)}, u32[]{:S(2)}, u32[]{:S(2)}) %all-to-all-start.1) | async-done | bytes 524320 | tf_op jit(solution)/shard_map/all_to_all | solution.py:97
  47.0 3.6 all-to-all-start
  50.6 2.4 collective-permute-start
  53.1 13.5 %collective-permute-done = bf16[128,2048]{1,0:T(8,128)(2,1)S(1)} collective-permute-done((bf16[128,2048]{1,0:T(8,128)(2,1)S(1)}, bf16[128,2048]{1,0:T(8,128)(2,1)S(1)}, u32[]{:S(2)}, u32[]{:S(2)}) %collective-permute-start) | collective-permute-done | bytes 524320 | tf_op jit(solution)/shard_map/ppermute | solution.py:14
  66.6 1.0 copy.53
  67.7 2.4 all-to-all-done
  70.1 11.9 %all-to-all-start.2 = ((bf16[128,16,128]{0,2,1:T(8,128)(2,1)}), bf16[128,16,128]{0,2,1:T(8,128)(2,1)}, u32[]{:S(2)}, u32[]{:S(2)}) async-start(bf16[128,16,128]{0,2,1:T(8,128)(2,1)} %bitcast.7), calls=%async_computation.2 | async-start | bytes 1048576 | tf_op jit(solution)/shard_map/all_to_all | solution.py:99
  85.6 1.0 fusion.61
  86.7 1.0 fusion.40
  89.1 2.7 fusion.2
  91.8 9.9 %all-to-all-done.2 = bf16[128,16,128]{0,2,1:T(8,128)(2,1)} async-done(((bf16[128,16,128]{0,2,1:T(8,128)(2,1)}), bf16[128,16,128]{0,2,1:T(8,128)(2,1)}, u32[]{:S(2)}, u32[]{:S(2)}) %all-to-all-start.2) | async-done | bytes 524320 | tf_op jit(solution)/shard_map/all_to_all | solution.py:99
  101.7 1.3 slice_bitcast_fusion.3
  103.0 1.4 fusion.47
  106.0 1.5 copy-done
  108.3 25.2 %all_to_all.128 = bf16[16,128,128]{2,1,0:T(8,128)(2,1)S(1)} all-to-all(bf16[16,128,128]{2,1,0:T(8,128)(2,1)S(1)} %bitcast.130), channel_id=1, replica_groups=mesh['dp'=8,'pipe'=4,'seq'=16] {'seq'}, dimensions={0} | all-to-all | bytes 1048576 | tf_op jit(solution)/shard_map/all_to_all | solution.py:108
  134.2 1.6 copy.65
  135.8 1.6 broadcast_in_dim.36
  139.3 5.5 all-to-all-start.3
  144.7 2.3 copy.66
  147.0 17.4 %all-to-all-done.3 = bf16[128,16,128]{2,0,1:T(8,128)(2,1)} async-done(((bf16[128,16,128]{2,0,1:T(8,128)(2,1)}), bf16[128,16,128]{2,0,1:T(8,128)(2,1)}, u32[]{:S(2)}, u32[]{:S(2)}) %all-to-all-start.3) | async-done | bytes 524320 | tf_op jit(solution)/shard_map/all_to_all | solution.py:98
  164.4 5.3 all-to-all-start.7
  170.4 1.0 slice.254
  171.4 1.0 slice.259
  172.4 1.0 slice.263
  173.4 1.4 fusion.30
  181.3 1.9 fusion.31
  183.8 1.1 copy-done.2
  185.7 2.0 multiply_convert_fusion
  187.7 1.3 copy-done.4
  189.1 1.6 fusion.13
  190.6 7.4 %all-to-all-done.7 = bf16[128,16,256]{0,2,1:T(8,128)(2,1)} async-done(((bf16[128,16,256]{0,2,1:T(8,128)(2,1)}), bf16[128,16,256]{0,2,1:T(8,128)(2,1)}, u32[]{:S(2)}, u32[]{:S(2)}) %all-to-all-start.7) | async-done | bytes 1048608 | tf_op jit(solution)/shard_map/all_to_all | solution.py:117
  198.1 10.7 %all-to-all-start.5 = ((bf16[16,128,128]{2,1,0:T(8,128)(2,1)}), bf16[16,128,128]{2,1,0:T(8,128)(2,1)}, u32[]{:S(2)}, u32[]{:S(2)}) async-start(bf16[16,128,128]{2,1,0:T(8,128)(2,1)} %bitcast.134), calls=%async_computation.5 | async-start | bytes 1048576 | tf_op jit(solution)/shard_map/all_to_all | solution.py:107
  208.8 1.4 fusion.24
  210.2 1.4 fusion.27
  213.8 42.3 %all-to-all-done.5 = bf16[16,128,128]{2,1,0:T(8,128)(2,1)} async-done(((bf16[16,128,128]{2,1,0:T(8,128)(2,1)}), bf16[16,128,128]{2,1,0:T(8,128)(2,1)}, u32[]{:S(2)}, u32[]{:S(2)}) %all-to-all-start.5) | async-done | bytes 524320 | tf_op jit(solution)/shard_map/all_to_all | solution.py:107
  256.1 9.1 %all-to-all-start.4 = ((bf16[16,128,128]{2,1,0:T(8,128)(2,1)}), bf16[16,128,128]{2,1,0:T(8,128)(2,1)S(1)}, u32[]{:S(2)}, u32[]{:S(2)}) async-start(bf16[16,128,128]{2,1,0:T(8,128)(2,1)} %bitcast.22), calls=%async_computation.4 | async-start | bytes 1048576 | tf_op jit(solution)/shard_map/all_to_all | solution.py:106
  265.2 1.5 copy.67
  266.7 1.1 bitcast_reduce_fusion.1
  268.8 25.7 %all-to-all-done.4 = bf16[16,128,128]{2,1,0:T(8,128)(2,1)S(1)} async-done(((bf16[16,128,128]{2,1,0:T(8,128)(2,1)}), bf16[16,128,128]{2,1,0:T(8,128)(2,1)S(1)}, u32[]{:S(2)}, u32[]{:S(2)}) %all-to-all-start.4) | async-done | bytes 524320 | tf_op jit(solution)/shard_map/all_to_all | solution.py:106
  294.8 1.0 broadcast_in_dim.71
  295.9 3.0 fusion.23
  298.9 122.1 %all-gather.6.cloned.1.call-done = bf16[1,4096,512]{2,1,0:T(8,128)(2,1)} async-done(((bf16[1,256,512]{2,1,0:T(8,128)(2,1)}), bf16[1,4096,512]{2,1,0:T(8,128)(2,1)}) %all-gather.6.cloned.1.call-update) | async-done | bytes 4194320 | tf_op jit(solution)/shard_map/all_gather | solution.py:125
  421.0 4.7 fusion
  425.7 115.2 %all-reduce.4.cloned.1.call-done = bf16[1,256,512]{1,2,0:T(8,128)(2,1)} async-done(((bf16[1,256,512]{1,2,0:T(8,128)(2,1)}), bf16[1,256,512]{1,2,0:T(8,128)(2,1)}) %all-reduce.4.cloned.1.call-update) | async-done | bytes 262160 | tf_op jit(solution)/shard_map/psum | solution.py:122
  540.9 1.9 copy.69
  (115 shorter events, 22.8 us)
Async XLA Ops:
  7.2 19.8 %copy-start.25 = (bf16[1,1,128,2048]{3,2,1,0:T(8,128)(2,1)S(1)}, bf16[1,1,128,2048]{3,2,1,0:T(8,128)(2,1)}, u32[]{:S(2)}) copy-start(bf16[1,1,128,2048]{3,2,1,0:T(8,128)(2,1)} %param.26) | copy-start | bytes 1572868
  8.2 42.4 %copy-start.33 = (bf16[1,1,128,2048]{3,2,1,0:T(8,128)(2,1)S(1)}, bf16[1,1,128,2048]{3,2,1,0:T(8,128)(2,1)}, u32[]{:S(2)}) copy-start(bf16[1,1,128,2048]{3,2,1,0:T(8,128)(2,1)} %param.29) | copy-start | bytes 1572868
  9.1 37.9 %all-to-all-start.1 = ((bf16[128,16,128]{2,0,1:T(8,128)(2,1)}), bf16[128,16,128]{2,0,1:T(8,128)(2,1)S(1)}, u32[]{:S(2)}, u32[]{:S(2)}) async-start(bf16[128,16,128]{2,0,1:T(8,128)(2,1)} %bitcast.3), calls=%async_computation.1 | async-start | bytes 1048576 | tf_op jit(solution)/shard_map/all_to_all | solution.py:97
  47.0 38.5 %copy-start.10 = (bf16[128,16,128]{2,0,1:T(8,128)(2,1)}, bf16[128,16,128]{2,0,1:T(8,128)(2,1)S(1)}, u32[]{:S(2)}) copy-start(bf16[128,16,128]{2,0,1:T(8,128)(2,1)S(1)} %all-to-all-done.1) | copy-start | bytes 1572868
  47.0 23.1 %all-to-all-start = ((bf16[128,16,128]{0,2,1:T(8,128)(2,1)}), bf16[128,16,128]{0,2,1:T(8,128)(2,1)S(1)}, u32[]{:S(2)}, u32[]{:S(2)}) async-start(bf16[128,16,128]{0,2,1:T(8,128)(2,1)} %bitcast), calls=%async_computation | async-start | bytes 1048576 | tf_op jit(solution)/shard_map/all_to_all | solution.py:96
  50.6 16.0 %collective-permute-start = (bf16[128,2048]{1,0:T(8,128)(2,1)S(1)}, bf16[128,2048]{1,0:T(8,128)(2,1)S(1)}, u32[]{:S(2)}, u32[]{:S(2)}) collective-permute-start(bf16[128,2048]{1,0:T(8,128)(2,1)S(1)} %bitcast.157), channel_id=1, source_target_pairs={{16,0},{32,16},{48,32},{0,48},{17,1},{33,17},{49,33},{1,49},{18,2}... | collective-permute-start | bytes 1572872 | tf_op jit(solution)/shard_map/ppermute | solution.py:14
  67.6 15.1 %copy-start.26 = (bf16[4,128,128]{2,1,0:T(8,128)(2,1)}, bf16[4,128,128]{2,1,0:T(8,128)(2,1)S(1)}, u32[]{:S(2)}) copy-start(bf16[4,128,128]{2,1,0:T(8,128)(2,1)S(1)} %slice.253) | copy-start | bytes 393220
  67.7 15.4 %copy-start.20 = (bf16[8,128,128]{2,1,0:T(8,128)(2,1)}, bf16[8,128,128]{2,1,0:T(8,128)(2,1)S(1)}, u32[]{:S(2)}) copy-start(bf16[8,128,128]{2,1,0:T(8,128)(2,1)S(1)} %slice.257) | copy-start | bytes 786436
  67.7 16.5 %copy-start.17 = (bf16[12,128,128]{2,1,0:T(8,128)(2,1)}, bf16[12,128,128]{2,1,0:T(8,128)(2,1)S(1)}, u32[]{:S(2)}) copy-start(bf16[12,128,128]{2,1,0:T(8,128)(2,1)S(1)} %slice.261) | copy-start | bytes 1179652
  70.1 31.5 %all-to-all-start.2 = ((bf16[128,16,128]{0,2,1:T(8,128)(2,1)}), bf16[128,16,128]{0,2,1:T(8,128)(2,1)}, u32[]{:S(2)}, u32[]{:S(2)}) async-start(bf16[128,16,128]{0,2,1:T(8,128)(2,1)} %bitcast.7), calls=%async_computation.2 | async-start | bytes 1048576 | tf_op jit(solution)/shard_map/all_to_all | solution.py:99
  82.0 213.8 %all-gather.4.cloned.1.call-start = ((), (), s32[]{:S(2)}) async-start(), calls=%async_computation.8 | async-start | bytes 2228224 | tf_op jit(solution)/shard_map/all_gather | solution.py:118
  82.3 1.4 copy-start.23
  82.4 3.1 copy-start.29
  82.7 1.5 copy-start.21
  83.0 3.7 copy-start.6
  83.7 1.3 copy-start.14
  101.7 2.8 copy-start.15
  103.0 1.5 copy-start.27
  103.0 2.3 copy-start.31
  105.3 2.2 copy-start
  139.3 25.1 %all-to-all-start.3 = ((bf16[128,16,128]{2,0,1:T(8,128)(2,1)}), bf16[128,16,128]{2,0,1:T(8,128)(2,1)}, u32[]{:S(2)}, u32[]{:S(2)}) async-start(bf16[128,16,128]{2,0,1:T(8,128)(2,1)} %bitcast.131), calls=%async_computation.3 | async-start | bytes 1048576 | tf_op jit(solution)/shard_map/all_to_all | solution.py:98
  164.4 33.7 %all-to-all-start.7 = ((bf16[128,16,256]{0,2,1:T(8,128)(2,1)}), bf16[128,16,256]{0,2,1:T(8,128)(2,1)}, u32[]{:S(2)}, u32[]{:S(2)}) async-start(bf16[128,16,256]{0,2,1:T(8,128)(2,1)} %bitcast.122), calls=%async_computation.7 | async-start | bytes 2097152 | tf_op jit(solution)/shard_map/all_to_all | solution.py:117
  169.6 251.4 %all-gather.6.cloned.1.call-start = ((), (), s32[]{:S(2)}) async-start(), calls=%async_computation.10 | async-start | bytes 4456448 | tf_op jit(solution)/shard_map/all_gather | solution.py:125
  170.4 4.4 copy-start.7
  170.4 4.4 copy-start.28
  174.8 1.1 copy-start.24
  175.2 0.8 copy-start.12
  176.3 1.6 copy-start.16
  176.3 1.6 copy-start.32
  178.6 0.9 copy-start.22
  178.6 2.6 copy-start.1
  179.5 1.0 copy-start.8
  183.8 1.2 copy-start.2
  185.7 3.4 copy-start.30
  187.7 1.4 copy-start.4
  189.1 19.7 %copy-start.13 = (bf16[512,512]{0,1:T(8,128)(2,1)S(1)}, bf16[512,512]{0,1:T(8,128)(2,1)}, u32[]{:S(2)}) copy-start(bf16[512,512]{0,1:T(8,128)(2,1)} %copy-done.12) | copy-start | bytes 1572868
  189.1 21.1 %copy-start.9 = (bf16[512,1024]{1,0:T(8,128)(2,1)S(1)}, bf16[512,1024]{1,0:T(8,128)(2,1)}, u32[]{:S(2)}) copy-start(bf16[512,1024]{1,0:T(8,128)(2,1)} %copy-done.8) | copy-start | bytes 3145732
  190.6 21.0 %copy-start.3 = (bf16[512,1536]{1,0:T(8,128)(2,1)S(1)}, bf16[512,1536]{1,0:T(8,128)(2,1)}, u32[]{:S(2)}) copy-start(bf16[512,1536]{1,0:T(8,128)(2,1)} %copy-done.2) | copy-start | bytes 4718596
  190.6 21.0 %copy-start.18 = (bf16[12,128,128]{2,1,0:T(8,128)(2,1)S(1)}, bf16[12,128,128]{2,1,0:T(8,128)(2,1)}, u32[]{:S(2)}) copy-start(bf16[12,128,128]{2,1,0:T(8,128)(2,1)} %copy-done.17) | copy-start | bytes 1179652
  198.1 58.0 %all-to-all-start.5 = ((bf16[16,128,128]{2,1,0:T(8,128)(2,1)}), bf16[16,128,128]{2,1,0:T(8,128)(2,1)}, u32[]{:S(2)}, u32[]{:S(2)}) async-start(bf16[16,128,128]{2,1,0:T(8,128)(2,1)} %bitcast.134), calls=%async_computation.5 | async-start | bytes 1048576 | tf_op jit(solution)/shard_map/all_to_all | solution.py:107
  208.8 3.4 copy-start.5
  208.8 3.4 copy-start.11
  256.1 38.4 %all-to-all-start.4 = ((bf16[16,128,128]{2,1,0:T(8,128)(2,1)}), bf16[16,128,128]{2,1,0:T(8,128)(2,1)S(1)}, u32[]{:S(2)}, u32[]{:S(2)}) async-start(bf16[16,128,128]{2,1,0:T(8,128)(2,1)} %bitcast.22), calls=%async_computation.4 | async-start | bytes 1048576 | tf_op jit(solution)/shard_map/all_to_all | solution.py:106
  265.2 275.7 %all-reduce.4.cloned.1.call-start = ((), (), s32[]{:S(2)}) async-start(), calls=%async_computation.9 | async-start | bytes 524288 | tf_op jit(solution)/shard_map/psum | solution.py:122
  295.9 125.2 %copy-start.19 = (bf16[128,4,128]{0,2,1:T(8,128)(2,1)S(1)}, bf16[128,4,128]{0,2,1:T(8,128)(2,1)}, u32[]{:S(2)}) copy-start(bf16[128,4,128]{0,2,1:T(8,128)(2,1)} %copy.65) | copy-start | bytes 393220
Sparse Core Ops, SparseCore 0:
  136.0 132.1 all-gather.3
  271.5 149.5 all-gather.5
  424.5 116.3 all-reduce.3
where the time goes:
time: 551 us; the launch traced here: 549 us
  waiting for transfers between devices  376 us (68%)
  starting transfers between devices  66.5 us (12%)
  matrix products  29.5 us (5%)
  local copies, waits for them, and re-layouts  29.1 us (5%)
  blocking collectives  25.2 us (5%)
  between operations  14.4 us (3%)
  other arithmetic  9.02 us (2%)
    all_gather x1, waiting for transfers between devices, local(): lax.all_gather(value_proj, 'seq', axis=0, tiled=True)  122 us
    psum x1, waiting for transfers between devices, local(): lax.psum(weight_term.astype(jnp.bfloat16), 'dp').astype(jnp.float32)  115 us
    all_to_all x1, waiting for transfers between devices, local(): lax.all_to_all(key_terms, 'seq', split_axis=0, concat_axis=1, tiled=True)  42.3 us
    all_to_all x1, waiting for transfers between devices, local(): lax.all_to_all(query_terms, 'seq', split_axis=0, concat_axis=1, tiled=True)  25.7 us
    all_to_all x1, blocking collectives, local(): lax.all_to_all(value_terms, 'seq', split_axis=0, concat_axis=1, tiled=True)  25.2 us
    all_to_all x1, waiting for transfers between devices, local(): lax.all_to_all(widen(key_rows), 'seq', split_axis=1, concat_axis=0, tiled...  19.1 us
    all_to_all x1, starting transfers between devices, local(): lax.all_to_all(widen(key_rows), 'seq', split_axis=1, concat_axis=0, tiled...  17.8 us
    all_to_all x1, waiting for transfers between devices, local(): lax.all_to_all(widen(value_rows), 'seq', split_axis=1, concat_axis=0, til...  17.4 us
  transfers between devices with their start and end apart: 11, of which 10 were waited for; matrix products, arithmetic and copies ran while one was open for 9% of the time, Pallas kernels for 0%

commit v1 on v0

--- a/solution.py
+++ b/solution.py
@@ -122,7 +122,9 @@
     weight_grad = lax.psum(weight_term.astype(jnp.bfloat16), "dp").astype(jnp.float32)
     full_rows = lax.dot_general(
         value_grad_rows,
-        lax.all_gather(value_proj, "seq", axis=0, tiled=True),
+        jnp.concatenate(
+            lax.all_to_all(jnp.stack([value_proj] * lax.axis_size("seq")), "seq", 0, 0), axis=0
+        ),
         (((1,), (1,)), ((), ())),
         preferred_element_type=jnp.float32,
     )

time: 551 us -> 647 us (1.17)
  waiting for transfers between devices: 376 us -> 462 us
    all_gather x1, waiting for transfers between devices: 0.01 us -> 228 us  [local(): all_value_grads = lax.all_gather(value_grad_rows, 'seq', axis=0, tiled=True)]
    all_gather x1 -> x0, waiting for transfers between devices: 122 us -> none  [local(): lax.all_gather(value_proj, 'seq', axis=0, tiled=True)]
    ppermute x1, waiting for transfers between devices: 13.5 us -> 0.01 us  [passed_along(): return lax.ppermute(block, axis, route)]
    all_to_all x1, waiting for transfers between devices: 2.41 us -> 15.7 us  [local(): lax.all_to_all(query_rows, 'seq', split_axis=1, concat_axis=0, tiled=True)]
    all_to_all x1, waiting for transfers between devices: 42.3 us -> 30.3 us  [local(): lax.all_to_all(key_terms, 'seq', split_axis=0, concat_axis=1, tiled=True)]
    all_to_all x1, waiting for transfers between devices: 25.7 us -> 14 us  [local(): lax.all_to_all(query_terms, 'seq', split_axis=0, concat_axis=1, tiled=True)]
    psum x1, waiting for transfers between devices: 115 us -> 126 us  [local(): lax.psum(weight_term.astype(jnp.bfloat16), 'dp').astype(jnp.float32)]
    all_to_all x0 -> x1, starting transfers between devices: none -> 6.86 us  [local(): lax.all_to_all(jnp.stack([value_proj] * lax.axis_size('seq')), 'seq', 0, 0)]
  transfers between devices with their start and end apart: 11 -> 11, of which waited for: 10 -> 9; matrix products, arithmetic and copies ran while one was open for 9% -> 8% of each run, Pallas kernels for 0% -> 0%
where the time goes in v1:
time: 647 us; the launch traced here: 646 us
  waiting for transfers between devices  462 us (71%)
  starting transfers between devices  71.2 us (11%)
  matrix products  31.2 us (5%)
  local copies, waits for them, and re-layouts  29 us (4%)
  blocking collectives  28 us (4%)
  between operations  14.8 us (2%)
  other arithmetic  9.06 us (1%)
    all_gather x1, waiting for transfers between devices, local(): all_value_grads = lax.all_gather(value_grad_rows, 'seq', axis=0, tiled=True)  228 us
    psum x1, waiting for transfers between devices, local(): lax.psum(weight_term.astype(jnp.bfloat16), 'dp').astype(jnp.float32)  126 us
    all_to_all x1, waiting for transfers between devices, local(): lax.all_to_all(key_terms, 'seq', split_axis=0, concat_axis=1, tiled=True)  30.3 us
    all_to_all x1, blocking collectives, local(): lax.all_to_all(value_terms, 'seq', split_axis=0, concat_axis=1, tiled=True)  28 us
    all_to_all x1, waiting for transfers between devices, local(): lax.all_to_all(widen(key_rows), 'seq', split_axis=1, concat_axis=0, tiled...  19.1 us
    all_to_all x1, starting transfers between devices, local(): lax.all_to_all(widen(key_rows), 'seq', split_axis=1, concat_axis=0, tiled...  17.8 us
    all_to_all x1, waiting for transfers between devices, local(): lax.all_to_all(query_rows, 'seq', split_axis=1, concat_axis=0, tiled=True)  15.7 us
    unnamed x105, local copies, waits for them, and re-layouts  15.7 us
  transfers between devices with their start and end apart: 11, of which 9 were waited for; matrix products, arithmetic and copies ran while one was open for 8% of the time, Pallas kernels for 0%

profile of v1, /device:TPU:2, one launch (start us, length us, event | category | flops | bytes accessed | tf_op | source)
XLA Modules:
  0.0 645.7 jit_solution(16145066822440414286)
XLA Ops:
  7.2 1.0 broadcast_in_dim.33
  8.2 0.9 broadcast_in_dim.34
  9.1 17.8 %all-to-all-start.1 = ((bf16[128,16,128]{2,0,1:T(8,128)(2,1)}), bf16[128,16,128]{2,0,1:T(8,128)(2,1)S(1)}, u32[]{:S(2)}, u32[]{:S(2)}) async-start(bf16[128,16,128]{2,0,1:T(8,128)(2,1)} %bitcast.3), calls=%async_computation.1 | async-start | bytes 1048576 | tf_op jit(solution)/shard_map/all_to_all | solution.py:97
  27.0 1.0 copy.50
  28.0 19.1 %all-to-all-done.1 = bf16[128,16,128]{2,0,1:T(8,128)(2,1)S(1)} async-done(((bf16[128,16,128]{2,0,1:T(8,128)(2,1)}), bf16[128,16,128]{2,0,1:T(8,128)(2,1)S(1)}, u32[]{:S(2)}, u32[]{:S(2)}) %all-to-all-start.1) | async-done | bytes 524320 | tf_op jit(solution)/shard_map/all_to_all | solution.py:97
  47.0 3.6 all-to-all-start
  50.6 2.4 collective-permute-start
  53.1 1.3 copy.66
  54.5 15.7 %all-to-all-done = bf16[128,16,128]{0,2,1:T(8,128)(2,1)S(1)} async-done(((bf16[128,16,128]{0,2,1:T(8,128)(2,1)}), bf16[128,16,128]{0,2,1:T(8,128)(2,1)S(1)}, u32[]{:S(2)}, u32[]{:S(2)}) %all-to-all-start) | async-done | bytes 524320 | tf_op jit(solution)/shard_map/all_to_all | solution.py:96
  71.0 7.6 %all-to-all-start.3 = ((bf16[128,16,128]{2,0,1:T(8,128)(2,1)}), bf16[128,16,128]{2,0,1:T(8,128)(2,1)S(1)}, u32[]{:S(2)}, u32[]{:S(2)}) async-start(bf16[128,16,128]{2,0,1:T(8,128)(2,1)} %bitcast.9), calls=%async_computation.3 | async-start | bytes 1048576 | tf_op jit(solution)/shard_map/all_to_all | solution.py:98
  78.7 1.0 copy.53
  81.0 1.2 fusion.15
  84.7 2.8 fusion.60
  87.5 10.7 %all-to-all-done.3 = bf16[128,16,128]{2,0,1:T(8,128)(2,1)S(1)} async-done(((bf16[128,16,128]{2,0,1:T(8,128)(2,1)}), bf16[128,16,128]{2,0,1:T(8,128)(2,1)S(1)}, u32[]{:S(2)}, u32[]{:S(2)}) %all-to-all-start.3) | async-done | bytes 524320 | tf_op jit(solution)/shard_map/all_to_all | solution.py:98
  98.2 9.3 %all-to-all-start.2 = ((bf16[128,16,128]{0,2,1:T(8,128)(2,1)}), bf16[128,16,128]{0,2,1:T(8,128)(2,1)}, u32[]{:S(2)}, u32[]{:S(2)}) async-start(bf16[128,16,128]{0,2,1:T(8,128)(2,1)} %bitcast.7), calls=%async_computation.2 | async-start | bytes 1048576 | tf_op jit(solution)/shard_map/all_to_all | solution.py:99
  109.2 0.9 fusion.39
  110.9 1.2 copy-done.6
  112.7 2.7 fusion.1
  115.4 11.8 %all-to-all-done.2 = bf16[128,16,128]{0,2,1:T(8,128)(2,1)} async-done(((bf16[128,16,128]{0,2,1:T(8,128)(2,1)}), bf16[128,16,128]{0,2,1:T(8,128)(2,1)}, u32[]{:S(2)}, u32[]{:S(2)}) %all-to-all-start.2) | async-done | bytes 524320 | tf_op jit(solution)/shard_map/all_to_all | solution.py:99
  127.2 6.2 all-to-all-start.8
  133.4 1.1 slice_bitcast_fusion.3
  134.5 1.5 fusion.29
  136.1 1.6 fusion.18
  145.6 1.1 copy-done.3
  147.4 0.9 multiply_convert_fusion
  148.4 1.4 copy-done.9
  149.8 1.6 fusion.12
  151.4 7.3 %all-to-all-done.8 = bf16[128,16,256]{0,2,1:T(8,128)(2,1)} async-done(((bf16[128,16,256]{0,2,1:T(8,128)(2,1)}), bf16[128,16,256]{0,2,1:T(8,128)(2,1)}, u32[]{:S(2)}, u32[]{:S(2)}) %all-to-all-start.8) | async-done | bytes 1048608 | tf_op jit(solution)/shard_map/all_to_all | solution.py:117
  158.7 9.9 %all-to-all-start.5 = ((bf16[16,128,128]{2,1,0:T(8,128)(2,1)}), bf16[16,128,128]{2,1,0:T(8,128)(2,1)}, u32[]{:S(2)}, u32[]{:S(2)}) async-start(bf16[16,128,128]{2,1,0:T(8,128)(2,1)} %bitcast.138), calls=%async_computation.5 | async-start | bytes 1048576 | tf_op jit(solution)/shard_map/all_to_all | solution.py:107
  168.6 1.6 fusion.23
  170.2 1.7 fusion.26
  174.1 30.3 %all-to-all-done.5 = bf16[16,128,128]{2,1,0:T(8,128)(2,1)} async-done(((bf16[16,128,128]{2,1,0:T(8,128)(2,1)}), bf16[16,128,128]{2,1,0:T(8,128)(2,1)}, u32[]{:S(2)}, u32[]{:S(2)}) %all-to-all-start.5) | async-done | bytes 524320 | tf_op jit(solution)/shard_map/all_to_all | solution.py:107
  204.3 7.2 %all-to-all-start.4 = ((bf16[16,128,128]{2,1,0:T(8,128)(2,1)}), bf16[16,128,128]{2,1,0:T(8,128)(2,1)}, u32[]{:S(2)}, u32[]{:S(2)}) async-start(bf16[16,128,128]{2,1,0:T(8,128)(2,1)} %bitcast.137), calls=%async_computation.4 | async-start | bytes 1048576 | tf_op jit(solution)/shard_map/all_to_all | solution.py:106
  211.6 1.5 fusion.46
  215.0 1.5 copy-done.1
  217.2 14.0 %all-to-all-done.4 = bf16[16,128,128]{2,1,0:T(8,128)(2,1)} async-done(((bf16[16,128,128]{2,1,0:T(8,128)(2,1)}), bf16[16,128,128]{2,1,0:T(8,128)(2,1)}, u32[]{:S(2)}, u32[]{:S(2)}) %all-to-all-start.4) | async-done | bytes 524320 | tf_op jit(solution)/shard_map/all_to_all | solution.py:106
  231.2 28.0 %all_to_all.133 = bf16[16,128,128]{2,1,0:T(8,128)(2,1)S(1)} all-to-all(bf16[16,128,128]{2,1,0:T(8,128)(2,1)S(1)} %bitcast.135), channel_id=1, replica_groups=mesh['dp'=8,'pipe'=4,'seq'=16] {'seq'}, dimensions={0} | all-to-all | bytes 1048576 | tf_op jit(solution)/shard_map/all_to_all | solution.py:108
  259.3 2.4 stack.3
  261.7 6.9 %all-to-all-start.7 = ((bf16[16,256,512]{2,1,0:T(8,128)(2,1)}), bf16[16,256,512]{2,1,0:T(8,128)(2,1)}, u32[]{:S(2)}, u32[]{:S(2)}) async-start(bf16[16,256,512]{2,1,0:T(8,128)(2,1)} %stack.3), calls=%async_computation.7 | async-start | bytes 8388608 | tf_op jit(solution)/shard_map/all_to_all | solution.py:126
  269.8 1.5 copy.67
  271.3 227.9 %all-gather.2.cloned.1.call-done = bf16[2048,512]{0,1:T(8,128)(2,1)} async-done(((bf16[128,512]{0,1:T(8,128)(2,1)}), bf16[2048,512]{0,1:T(8,128)(2,1)}) %all-gather.2.cloned.1.call-update) | async-done | bytes 2097168 | tf_op jit(solution)/shard_map/all_gather | solution.py:118
  499.1 3.0 fusion.22
  502.2 1.1 bitcast_reduce_fusion.1
  504.3 1.4 copy.63
  505.6 1.0 broadcast_in_dim.71
  506.7 125.6 %all-reduce.4.cloned.1.call-done = bf16[1,256,512]{1,2,0:T(8,128)(2,1)} async-done(((bf16[1,256,512]{1,2,0:T(8,128)(2,1)}), bf16[1,256,512]{1,2,0:T(8,128)(2,1)}) %all-reduce.4.cloned.1.call-update) | async-done | bytes 262160 | tf_op jit(solution)/shard_map/psum | solution.py:122
  632.3 1.9 copy.69
  634.2 4.7 fusion
  (147 shorter events, 22.9 us)
Async XLA Ops:
  7.2 19.8 %copy-start.34 = (bf16[1,1,128,2048]{3,2,1,0:T(8,128)(2,1)S(1)}, bf16[1,1,128,2048]{3,2,1,0:T(8,128)(2,1)}, u32[]{:S(2)}) copy-start(bf16[1,1,128,2048]{3,2,1,0:T(8,128)(2,1)} %param.26) | copy-start | bytes 1572868
  8.2 44.9 %copy-start.42 = (bf16[1,1,128,512]{3,2,1,0:T(8,128)(2,1)S(1)}, bf16[1,1,128,512]{3,2,1,0:T(8,128)(2,1)}, u32[]{:S(2)}) copy-start(bf16[1,1,128,512]{3,2,1,0:T(8,128)(2,1)} %param.28) | copy-start | bytes 393220
  8.2 44.9 %copy-start.26 = (bf16[1,1,128,4096]{3,2,1,0:T(8,128)(2,1)S(1)}, bf16[1,1,128,4096]{3,2,1,0:T(8,128)(2,1)}, u32[]{:S(2)}) copy-start(bf16[1,1,128,4096]{3,2,1,0:T(8,128)(2,1)} %param.30) | copy-start | bytes 3145732
  9.1 37.9 %all-to-all-start.1 = ((bf16[128,16,128]{2,0,1:T(8,128)(2,1)}), bf16[128,16,128]{2,0,1:T(8,128)(2,1)S(1)}, u32[]{:S(2)}, u32[]{:S(2)}) async-start(bf16[128,16,128]{2,0,1:T(8,128)(2,1)} %bitcast.3), calls=%async_computation.1 | async-start | bytes 1048576 | tf_op jit(solution)/shard_map/all_to_all | solution.py:97
  47.0 37.7 %copy-start.13 = (bf16[128,16,128]{2,0,1:T(8,128)(2,1)}, bf16[128,16,128]{2,0,1:T(8,128)(2,1)S(1)}, u32[]{:S(2)}) copy-start(bf16[128,16,128]{2,0,1:T(8,128)(2,1)S(1)} %all-to-all-done.1) | copy-start | bytes 1572868
  47.0 23.1 %all-to-all-start = ((bf16[128,16,128]{0,2,1:T(8,128)(2,1)}), bf16[128,16,128]{0,2,1:T(8,128)(2,1)S(1)}, u32[]{:S(2)}, u32[]{:S(2)}) async-start(bf16[128,16,128]{0,2,1:T(8,128)(2,1)} %bitcast), calls=%async_computation | async-start | bytes 1048576 | tf_op jit(solution)/shard_map/all_to_all | solution.py:96
  50.6 28.0 %collective-permute-start = (bf16[128,2048]{1,0:T(8,128)(2,1)}, bf16[128,2048]{1,0:T(8,128)(2,1)S(1)}, u32[]{:S(2)}, u32[]{:S(2)}) collective-permute-start(bf16[128,2048]{1,0:T(8,128)(2,1)} %bitcast.162), channel_id=1, source_target_pairs={{16,0},{32,16},{48,32},{0,48},{17,1},{33,17},{49,33},{1,49},{18,2}... | collective-permute-start | bytes 1572872 | tf_op jit(solution)/shard_map/ppermute | solution.py:14
  71.0 27.2 %all-to-all-start.3 = ((bf16[128,16,128]{2,0,1:T(8,128)(2,1)}), bf16[128,16,128]{2,0,1:T(8,128)(2,1)S(1)}, u32[]{:S(2)}, u32[]{:S(2)}) async-start(bf16[128,16,128]{2,0,1:T(8,128)(2,1)} %bitcast.9), calls=%async_computation.3 | async-start | bytes 1048576 | tf_op jit(solution)/shard_map/all_to_all | solution.py:98
  79.7 3.9 copy-start.35
  79.7 2.5 copy-start.23
  79.9 3.7 copy-start.32
  80.1 4.6 copy-start.38
  80.2 2.0 copy-start.28
  80.4 1.9 copy-start.30
  81.0 2.0 copy-start.16
  81.0 2.0 copy-start.47
  83.0 1.7 copy-start.5
  84.7 24.5 %copy-start.11 = (f32[512,512]{0,1:T(8,128)}, f32[512,512]{0,1:T(8,128)S(1)}, u32[]{:S(2)}) copy-start(f32[512,512]{0,1:T(8,128)S(1)} %get-tuple-element.151) | copy-start | bytes 3145732
  87.5 22.6 %copy-start.45 = (f32[512]{0:T(512)}, f32[512]{0:T(512)S(1)}, u32[]{:S(2)}) copy-start(f32[512]{0:T(512)S(1)} %get-tuple-element.144) | copy-start | bytes 6148
  98.2 12.0 %copy-start.7 = (bf16[128,16,128]{2,0,1:T(8,128)(2,1)}, bf16[128,16,128]{2,0,1:T(8,128)(2,1)S(1)}, u32[]{:S(2)}) copy-start(bf16[128,16,128]{2,0,1:T(8,128)(2,1)S(1)} %all-to-all-done.3) | copy-start | bytes 1572868
  98.2 29.0 %all-to-all-start.2 = ((bf16[128,16,128]{0,2,1:T(8,128)(2,1)}), bf16[128,16,128]{0,2,1:T(8,128)(2,1)}, u32[]{:S(2)}, u32[]{:S(2)}) async-start(bf16[128,16,128]{0,2,1:T(8,128)(2,1)} %bitcast.7), calls=%async_computation.2 | async-start | bytes 1048576 | tf_op jit(solution)/shard_map/all_to_all | solution.py:99
  107.6 2.6 copy-start.2
  110.2 1.9 copy-start.6
  127.2 31.5 %all-to-all-start.8 = ((bf16[128,16,256]{0,2,1:T(8,128)(2,1)}), bf16[128,16,256]{0,2,1:T(8,128)(2,1)}, u32[]{:S(2)}, u32[]{:S(2)}) async-start(bf16[128,16,256]{0,2,1:T(8,128)(2,1)} %bitcast.127), calls=%async_computation.8 | async-start | bytes 2097152 | tf_op jit(solution)/shard_map/all_to_all | solution.py:117
  134.5 6.7 %copy-start.43 = (bf16[4,16,8,128]{3,2,1,0:T(8,128)(2,1)}, bf16[4,16,8,128]{3,2,1,0:T(8,128)(2,1)S(1)}, u32[]{:S(2)}) copy-start(bf16[4,16,8,128]{3,2,1,0:T(8,128)(2,1)S(1)} %get-tuple-element.139) | copy-start | bytes 393220
  134.5 10.4 %copy-start.21 = (bf16[4,16,8,128]{3,2,1,0:T(8,128)(2,1)}, bf16[4,16,8,128]{3,2,1,0:T(8,128)(2,1)S(1)}, u32[]{:S(2)}) copy-start(bf16[4,16,8,128]{3,2,1,0:T(8,128)(2,1)S(1)} %get-tuple-element.138) | copy-start | bytes 393220
  134.5 12.9 %copy-start.19 = (bf16[4,16,8,128]{3,2,1,0:T(8,128)(2,1)}, bf16[4,16,8,128]{3,2,1,0:T(8,128)(2,1)S(1)}, u32[]{:S(2)}) copy-start(bf16[4,16,8,128]{3,2,1,0:T(8,128)(2,1)S(1)} %get-tuple-element.137) | copy-start | bytes 393220
  136.1 2.5 copy-start.33
  141.2 2.6 copy-start
  142.1 1.9 copy-start.8
  144.9 1.8 copy-start.29
  147.4 2.3 copy-start.39
  151.4 20.5 %copy-start.24 = (bf16[12,128,128]{2,1,0:T(8,128)(2,1)S(1)}, bf16[12,128,128]{2,1,0:T(8,128)(2,1)}, u32[]{:S(2)}) copy-start(bf16[12,128,128]{2,1,0:T(8,128)(2,1)} %copy-done.23) | copy-start | bytes 1179652
  158.7 45.7 %all-to-all-start.5 = ((bf16[16,128,128]{2,1,0:T(8,128)(2,1)}), bf16[16,128,128]{2,1,0:T(8,128)(2,1)}, u32[]{:S(2)}, u32[]{:S(2)}) async-start(bf16[16,128,128]{2,1,0:T(8,128)(2,1)} %bitcast.138), calls=%async_computation.5 | async-start | bytes 1048576 | tf_op jit(solution)/shard_map/all_to_all | solution.py:107
  168.6 3.3 copy-start.4
  168.6 3.9 copy-start.10
  168.6 3.9 copy-start.14
  172.5 39.1 %copy-start.37 = (bf16[4,16,8,128]{3,2,1,0:T(8,128)(2,1)S(1)}, bf16[4,16,8,128]{3,2,1,0:T(8,128)(2,1)}, u32[]{:S(2)}) copy-start(bf16[4,16,8,128]{3,2,1,0:T(8,128)(2,1)} %copy-done.36) | copy-start | bytes 393220
  173.2 40.0 %copy-start.44 = (bf16[4,16,8,128]{3,2,1,0:T(8,128)(2,1)S(1)}, bf16[4,16,8,128]{3,2,1,0:T(8,128)(2,1)}, u32[]{:S(2)}) copy-start(bf16[4,16,8,128]{3,2,1,0:T(8,128)(2,1)} %copy-done.43) | copy-start | bytes 393220
  204.3 26.9 %all-to-all-start.4 = ((bf16[16,128,128]{2,1,0:T(8,128)(2,1)}), bf16[16,128,128]{2,1,0:T(8,128)(2,1)}, u32[]{:S(2)}, u32[]{:S(2)}) async-start(bf16[16,128,128]{2,1,0:T(8,128)(2,1)} %bitcast.137), calls=%async_computation.4 | async-start | bytes 1048576 | tf_op jit(solution)/shard_map/all_to_all | solution.py:106
  211.6 1.7 copy-start.18
  214.3 2.2 copy-start.1
  214.3 2.2 copy-start.20
  216.5 42.8 %copy-start.40 = (bf16[1,256,512]{2,1,0:T(8,128)(2,1)S(1)}, bf16[1,256,512]{2,1,0:T(8,128)(2,1)}, u32[]{:S(2)}) copy-start(bf16[1,256,512]{2,1,0:T(8,128)(2,1)} %param.31) | copy-start | bytes 786436
  261.7 372.5 %all-to-all-start.7 = ((bf16[16,256,512]{2,1,0:T(8,128)(2,1)}), bf16[16,256,512]{2,1,0:T(8,128)(2,1)}, u32[]{:S(2)}, u32[]{:S(2)}) async-start(bf16[16,256,512]{2,1,0:T(8,128)(2,1)} %stack.3), calls=%async_computation.7 | async-start | bytes 8388608 | tf_op jit(solution)/shard_map/all_to_all | solution.py:126
  268.6 230.6 %all-gather.2.cloned.1.call-start = ((), (), s32[]{:S(2)}) async-start(), calls=%async_computation.9 | async-start | bytes 2228224 | tf_op jit(solution)/shard_map/all_gather | solution.py:118
  269.5 362.8 %all-reduce.4.cloned.1.call-start = ((), (), s32[]{:S(2)}) async-start(), calls=%async_computation.10 | async-start | bytes 524288 | tf_op jit(solution)/shard_map/psum | solution.py:122
  502.2 132.0 %copy-start.25 = (bf16[128,4,128]{0,2,1:T(8,128)(2,1)S(1)}, bf16[128,4,128]{0,2,1:T(8,128)(2,1)}, u32[]{:S(2)}) copy-start(bf16[128,4,128]{0,2,1:T(8,128)(2,1)} %copy.65) | copy-start | bytes 393220
  (13 other events, 15.9 us)
Sparse Core Ops, SparseCore 0:
  273.1 225.9 all-gather.1
  502.6 129.6 all-reduce.3
